TPU v7x, 512 devices: a whole 4x4x16 slice. The times are simulated.
512 devices in a mesh: gy: 32 (over y_hi, z), gz: 16 (over y_lo, x, core).
Axes of the slice: x: 4, y: 4 (y_hi: 2, y_lo: 2; y = y_hi * 2 + y_lo), z: 16, core: 2. Of those that a mesh axis runs over, the one named last changes fastest.
Arguments:
- tokens: bfloat16 [2, 64, 32, 32, 1024], P(None, None, 'gy', 'gz'), may hold values from -64 to 64
- w_qkv: bfloat16 [1024, 3072], P('gy'), may hold values from -2 to 2
- w_out: bfloat16 [1024, 1024], P('gy'), may hold values from -0.1875 to 0.1875
- bias_x: float32 [16, 127], replicated, may hold values from -4 to 4
- bias_y: float32 [16, 63], replicated, may hold values from -4 to 4
- bias_z: float32 [16, 63], replicated, may hold values from -4 to 4
Outputs:
- mixed: bfloat16 [2, 64, 32, 32, 1024], P(None, None, 'gy', 'gz')
All inputs are finite; a program needn't handle non-finite values.
Results may differ from a plain program's by a relative error of at most 0.0083.
Values may be sent and summed in bfloat16 or wider, within the bound.
No kernel may reach another device: no remote copies, remote signals or barrier semaphores. Data moves between devices by JAX's collectives and lax.ppermute only.
A program may use at most 64 MiB of HBM per device.

v0:
```python
import jax
import jax.numpy as jnp
from jax import lax
from jax.sharding import Mesh
from jax.sharding import PartitionSpec as P

HEADS = 16
HEAD = 64
GY = ("gy_0", "gy_1")
einsum_forms = {
    1: ("bxyzhs,bwyzhs->byzhxw", "byzhxw,bwyzhs->bxyzhs"),
    2: ("bxyzhs,bxwzhs->bxzhyw", "bxzhyw,bxwzhs->bxyzhs"),
    3: ("bxyzhs,bxywhs->bxyhzw", "bxyhzw,bxywhs->bxyzhs"),
}


def laid_out(tiles, dim):
    tiles = jnp.moveaxis(tiles, 0, dim)
    shape = tiles.shape
    return tiles.reshape(*shape[:dim], shape[dim] * shape[dim + 1], *shape[dim + 2 :])


def stacked_from(shard, axes, sequence):
    tiles = shard[None]
    for k in sequence:
        tiles = lax.all_gather(tiles, axes[k], axis=0, tiled=True)
    held = [lax.axis_size(axes[k]) for k in reversed(sequence)]
    tiles = tiles.reshape(*held, *shard.shape)
    turned = sorted(range(len(sequence)), key=lambda place: sequence[len(sequence) - 1 - place])
    return tiles.transpose(*turned, *range(len(sequence), tiles.ndim)).reshape(-1, *shard.shape)


def gathered_by_axis(shard, axes, sequence, dim):
    return laid_out(stacked_from(shard, axes, sequence), dim)


def grouped_exchange(shard, axis, split_dim, concat_dim, work, item_dim, out_dim):

    def moved(group):
        return lax.all_to_all(group, axis, split_axis=split_dim, concat_axis=concat_dim, tiled=True)

    items = jax.tree.leaves(shard)[0].shape[item_dim]
    ends = [items * k // 2 for k in range(2 + 1)] if items % 2 == 0 else [0, items]
    groups = [
        jax.tree.map(lambda a: lax.slice_in_dim(a, low, high, axis=item_dim), shard)
        for low, high in zip(ends, ends[1:])
    ]
    arrived = [moved(group) for group in groups]
    made = [work(group) for group in arrived]
    return jax.tree.map(lambda *parts: jnp.concatenate(parts, axis=out_dim), *made)


def norm_rows(tokens):
    values = tokens.astype(jnp.float32)
    center = jnp.mean(values, axis=-1, keepdims=True)
    spread = jnp.mean((values - center) ** 2, axis=-1, keepdims=True)
    return ((values - center) * lax.rsqrt(spread + 1e-05)).astype(jnp.bfloat16)


def rel_bias(table):
    length = (table.shape[1] + 1) // 2
    offsets = (
        lax.broadcasted_iota(jnp.int32, (length, length), 0)
        - lax.broadcasted_iota(jnp.int32, (length, length), 1)
        + length
        - 1
    )
    lookup = (
        offsets[:, :, None] == lax.broadcasted_iota(jnp.int32, (1, 1, 2 * length - 1), 2)
    ).astype(jnp.float32)
    return jnp.einsum("hr,ijr->hij", table, lookup, precision=lax.Precision.HIGHEST)


def attend(qkv, table, axis):
    dims = qkv.shape
    features = dims[-1] // 3
    parts = qkv.reshape(dims[:-1] + (3, HEADS, HEAD))
    query = parts[..., 0, :, :]
    keys = parts[..., 1, :, :]
    values = parts[..., 2, :, :]
    score_form, mix_form = einsum_forms[axis]
    scores = jnp.einsum(score_form, query, keys, preferred_element_type=jnp.float32) * HEAD ** (
        -0.5
    ) + rel_bias(table)
    scores = scores - jnp.max(scores, axis=-1, keepdims=True)
    expo = jnp.exp(scores)
    weights = (expo / jnp.sum(expo, axis=-1, keepdims=True)).astype(jnp.bfloat16)
    mixed = jnp.einsum(mix_form, weights, values, preferred_element_type=jnp.float32)
    return mixed.reshape(dims[:-1] + (features,)).astype(jnp.bfloat16)


def return_y(result):
    return lax.all_to_all(result, GY, split_axis=2, concat_axis=1, tiled=True)


def return_z(result):
    return lax.all_to_all(result, "gz", split_axis=3, concat_axis=1, tiled=True)


def shards(tokens, w_qkv, w_out, bias_x, bias_y, bias_z):
    samples, depth, rows_y, rows_z, features = tokens.shape
    normed = norm_rows(tokens)
    gathered = gathered_by_axis(w_qkv, GY, (0, 1), 0)

    def project(inputs):
        product = jnp.dot(
            inputs.reshape(-1, features), gathered, preferred_element_type=jnp.float32
        )
        return product.astype(jnp.bfloat16).reshape(inputs.shape[:-1] + (3 * features,))

    def z_attention_inputs(lines):
        return return_z(attend(project(lines), bias_z, 3))

    along_x = attend(project(normed), bias_x, 1)
    along_y = return_y(
        attend(
            project(lax.all_to_all(normed, GY, split_axis=1, concat_axis=2, tiled=True)), bias_y, 2
        )
    )
    along_z = grouped_exchange(normed, "gz", 1, 3, z_attention_inputs, 0, 0)
    summed = along_x.astype(jnp.float32) + along_y.astype(jnp.float32) + along_z.astype(jnp.float32)
    summed = summed.astype(jnp.bfloat16).reshape(-1, features)
    residual = tokens.reshape(-1, features).astype(jnp.float32)
    result = residual + jnp.dot(
        summed, gathered_by_axis(w_out, GY, (0, 1), 0), preferred_element_type=jnp.float32
    )
    return result.astype(jnp.bfloat16).reshape(tokens.shape)


def solution(mesh):
    torus = Mesh(mesh.devices.reshape(2, 16, mesh.shape["gz"]), ("gy_0", "gy_1", "gz"))
    in_specs = (P(None, None, GY, "gz", None), P(GY, None), P(GY, None), P(), P(), P())
    out_specs = P(None, None, GY, "gz", None)
    return jax.shard_map(
        shards, mesh=torus, in_specs=in_specs, out_specs=out_specs, check_vma=False
    )
```

profile of v0, /device:TPU:1, one launch (start us, length us, event | category | flops | bytes accessed | tf_op | source)
XLA Modules:
  0.0 258.1 jit_solution(5049971114567313379)
XLA Ops:
  6.5 9.5 %all-gather = bf16[64,3072]{1,0:T(8,128)(2,1)} all-gather(bf16[32,3072]{1,0:T(8,128)(2,1)} %param.7), channel_id=2, replica_groups=mesh['gy_0'=2,'gy_1'=16,'gz'=16] {'gy_0'}, dimensions={0}, use_global_device_ids=true | all-gather | bytes 589824 | tf_op jit(solution)/shard_map/all_gather | solution.py:26
  16.1 1.6 convert_reduce_fusion
  17.7 1.9 multiply_reduce_fusion
  19.7 1.4 multiply_convert_fusion
  21.1 1.4 fusion.45
  22.5 15.3 %all_to_all.84 = bf16[1,64,1,2,1024]{4,3,2,0,1:T(2,128)(2,1)S(1)} all-to-all(bf16[1,64,1,2,1024]{4,3,2,0,1:T(2,128)(2,1)S(1)} %get-tuple-element.17), channel_id=1, replica_groups=mesh['gy_0'=2,'gy_1'=16,'gz'=16] {'gz'}, dimensions={1} | all-to-all | bytes 524288 | tf_op jit(solution)/shard_map/all_to_all | solution.py:40
  37.9 10.5 %all_to_all.85 = bf16[1,64,1,2,1024]{4,3,2,0,1:T(2,128)(2,1)S(1)} all-to-all(bf16[1,64,1,2,1024]{4,3,2,0,1:T(2,128)(2,1)S(1)} %get-tuple-element.18), channel_id=1, replica_groups=mesh['gy_0'=2,'gy_1'=16,'gz'=16] {'gz'}, dimensions={1} | all-to-all | bytes 524288 | tf_op jit(solution)/shard_map/all_to_all | solution.py:40
  48.3 15.8 %all-to-all-start = ((bf16[2,64,1,2,1024]{4,3,2,0,1:T(2,128)(2,1)}), bf16[2,64,1,2,1024]{4,3,2,0,1:T(2,128)(2,1)S(1)}, u32[]{:S(2)}, u32[]{:S(2)}) async-start(bf16[2,64,1,2,1024]{4,3,2,0,1:T(2,128)(2,1)} %multiply_convert_fusion), calls=%async_computation | async-start | bytes 1048576 | tf_op jit(solution)/shard_map/all_to_all | solution.py:117
  64.1 5.4 %all-gather.1 = bf16[64,1024]{1,0:T(8,128)(2,1)} all-gather(bf16[32,1024]{1,0:T(8,128)(2,1)S(1)} %copy-done.12), channel_id=3, replica_groups=mesh['gy_0'=2,'gy_1'=16,'gz'=16] {'gy_0'}, dimensions={0}, use_global_device_ids=true | all-gather | bytes 196608 | tf_op jit(solution)/shard_map/all_gather | solution.py:26
  69.6 1.2 convolution_bitcast_fusion
  71.0 1.2 convolution_bitcast_fusion.1
  72.2 0.9 copy.152
  73.6 28.8 %all-to-all-done = bf16[2,64,1,2,1024]{4,3,2,0,1:T(2,128)(2,1)S(1)} async-done(((bf16[2,64,1,2,1024]{4,3,2,0,1:T(2,128)(2,1)}), bf16[2,64,1,2,1024]{4,3,2,0,1:T(2,128)(2,1)S(1)}, u32[]{:S(2)}, u32[]{:S(2)}) %all-to-all-start) | async-done | bytes 524320 | tf_op jit(solution)/shard_map/all_to_all | solution.py:117
  102.5 0.4 copy.271
  103.0 24.8 %all-gather.5.cloned.1.call-done = bf16[32,32,3072]{2,1,0:T(8,128)(2,1)} async-done(((bf16[2,32,3072]{2,1,0:T(8,128)(2,1)}), bf16[32,32,3072]{2,1,0:T(8,128)(2,1)}) %all-gather.5.cloned.1.call-update) | async-done | bytes 6291472 | tf_op jit(solution)/shard_map/all_gather | solution.py:26
  127.9 3.2 %copy.142 = bf16[2,16,32,3072]{3,2,1,0:T(8,128)(2,1)S(1)} copy(bf16[2,16,32,3072]{3,2,0,1:T(8,128)(2,1)} %bitcast.195) | data formatting | bytes 12582912 | tf_op jit(solution)/shard_map/transpose | solution.py:30
  131.1 2.7 %copy-done.1 = bf16[2,16,32,3072]{3,2,1,0:T(8,128)(2,1)} copy-done((bf16[2,16,32,3072]{3,2,1,0:T(8,128)(2,1)}, bf16[2,16,32,3072]{3,2,1,0:T(8,128)(2,1)S(1)}, u32[]{:S(2)}) %copy-start.1) | copy-done | bytes 6291480
  133.8 1.0 convolution_convert_fusion.3
  134.8 1.0 reshape_reshape.21
  135.8 1.3 fusion.43
  137.1 2.8 %fusion.48 = (f32[4,16,32]{2,1,0:T(8,128)S(1)}, f32[4,16,32,32]{2,3,1,0:T(8,128)}) fusion(bf16[1,4,1,32,1,16,64]{6,5,4,3,1,2,0:T(8,128)(2,1)} %get-tuple-element.13, bf16[1,4,1,32,1,16,64]{6,5,4,3,1,2,0:T(8,128)(2,1)} %get-tuple-element.12, f32[16,32,32]{1,2,0:T(8,128)S(1)} %copy.162), kind=kOutput, calls=%fused_computation.95 | convolution fusion | flops 8650783 | bytes 860160 | tf_op jit(solution)/shard_map/sub | solution.py:85
  140.0 1.6 fusion.20
  141.8 1.0 reshape.299
  142.8 8.2 %all-to-all-start.3 = ((bf16[1,4,1,32,1024]{4,1,2,0,3:T(4,128)(2,1)}), bf16[1,4,1,32,1024]{4,1,2,0,3:T(4,128)(2,1)S(1)}, u32[]{:S(2)}, u32[]{:S(2)}) async-start(bf16[1,4,1,32,1024]{4,1,2,0,3:T(4,128)(2,1)} %reshape.299), calls=%async_computation.3 | async-start | bytes 524288 | tf_op jit(solution)/shard_map/all_to_all | solution.py:97
  151.0 3.8 %convolution_convert_fusion.2 = bf16[128,3072]{1,0:T(8,128)(2,1)S(1)} fusion(bf16[128,1024]{1,0:T(8,128)(2,1)S(1)} %reshape.283, bf16[1024,3072]{1,0:T(8,128)(2,1)} %bitcast.191), kind=kOutput, calls=%fused_computation.6 | convolution fusion | flops 805699584 | bytes 7340032 | tf_op jit(solution)/shard_map/dot_general | solution.py:106
  154.8 1.0 reshape_reshape.22
  155.9 1.2 fusion.44
  157.0 2.8 %fusion.47 = (f32[4,16,32]{2,1,0:T(8,128)S(1)}, f32[4,16,32,32]{2,3,1,0:T(8,128)}) fusion(bf16[1,4,1,32,1,16,64]{6,5,4,3,1,2,0:T(8,128)(2,1)} %get-tuple-element.16, bf16[1,4,1,32,1,16,64]{6,5,4,3,1,2,0:T(8,128)(2,1)S(1)} %get-tuple-element.15, f32[16,32,32]{1,2,0:T(8,128)} %copy-done.11), kind=kOutput, calls=%fused_computation.94 | convolution fusion | flops 8650783 | bytes 860160 | tf_op jit(solution)/shard_map/sub | solution.py:85
  159.8 1.6 fusion.21
  161.6 1.0 reshape.300
  162.6 5.8 %convolution_convert_fusion = bf16[256,3072]{1,0:T(8,128)(2,1)} fusion(bf16[256,1024]{1,0:T(8,128)(2,1)S(1)} %reshape.278, bf16[1024,3072]{1,0:T(8,128)(2,1)} %bitcast.192), kind=kOutput, calls=%fused_computation.4 | convolution fusion | flops 1611399168 | bytes 8388608 | tf_op jit(solution)/shard_map/dot_general | solution.py:106
  168.4 3.6 %reshape_reshape.20 = bf16[2,2,32,2,3,16,64]{6,5,4,3,2,1,0:T(8,128)(2,1)S(1)} reshape(bf16[256,3072]{1,0:T(8,128)(2,1)} %convolution_convert_fusion) | data formatting | bytes 3145728 | tf_op jit(solution)/shard_map/reshape;reshape | solution.py:77
  172.1 2.0 fusion.42
  174.0 4.3 %fusion.46 = (f32[2,2,2,16,32]{4,3,2,1,0:T(8,128)S(1)}, f32[2,2,2,16,32,32]{4,5,3,2,1,0:T(8,128)}) fusion(f32[16,32,32]{1,2,0:T(8,128)} %copy.152, bf16[2,2,32,2,1,16,64]{6,5,4,3,2,1,0:T(8,128)(2,1)} %get-tuple-element.10, bf16[2,2,32,2,1,16,64]{6,5,4,3,2,1,0:T(8,128)(2,1)} %get-tuple-element.9), kind=kOutput, calls=%fused_computation.93 | convolution fusion | flops 17301536 | bytes 1654784 | tf_op jit(solution)/shard_map/sub | solution.py:85
  178.3 5.7 %all-to-all-start.5 = ((bf16[1,4,1,32,1024]{4,1,2,0,3:T(4,128)(2,1)}), bf16[1,4,1,32,1024]{4,1,2,0,3:T(4,128)(2,1)S(1)}, u32[]{:S(2)}, u32[]{:S(2)}) async-start(bf16[1,4,1,32,1024]{4,1,2,0,3:T(4,128)(2,1)} %reshape.300), calls=%async_computation.5 | async-start | bytes 524288 | tf_op jit(solution)/shard_map/all_to_all | solution.py:97
  184.0 2.3 fusion.13
  186.3 0.4 copy.184
  186.8 1.4 reshape.298
  188.1 3.1 %all-to-all-done.5 = bf16[1,4,1,32,1024]{4,1,2,0,3:T(4,128)(2,1)S(1)} async-done(((bf16[1,4,1,32,1024]{4,1,2,0,3:T(4,128)(2,1)}), bf16[1,4,1,32,1024]{4,1,2,0,3:T(4,128)(2,1)S(1)}, u32[]{:S(2)}, u32[]{:S(2)}) %all-to-all-start.5) | async-done | bytes 262176 | tf_op jit(solution)/shard_map/all_to_all | solution.py:97
  191.2 9.9 %all-to-all-start.1 = ((bf16[2,2,32,2,1024]{4,3,1,0,2:T(2,128)(2,1)}), bf16[2,2,32,2,1024]{4,3,1,0,2:T(2,128)(2,1)}, u32[]{:S(2)}, u32[]{:S(2)}) async-start(bf16[2,2,32,2,1024]{4,3,1,0,2:T(2,128)(2,1)} %reshape.298), calls=%async_computation.1 | async-start | bytes 1048576 | tf_op jit(solution)/shard_map/all_to_all | solution.py:93
  201.1 1.5 copy.141
  202.8 3.2 %fusion.19 = f32[16,64,64]{2,0,1:T(8,128)S(1)} fusion(s32[64,64]{1,0:T(8,128)S(1)} %subtract_add_fusion, f32[16,127]{1,0:T(8,128)S(1)} %copy-done), kind=kOutput, calls=%fused_computation.38 | convolution fusion | flops 100397056 | bytes 286656 | tf_op jit(solution)/shard_map/hr,ijr->hij/dot_general | solution.py:71
  206.0 1.1 copy.146
  207.0 0.6 copy_convert_fusion
  207.7 1.7 reshape.289
  209.4 3.2 %copy.178 = bf16[2,16,32,1024]{3,2,1,0:T(8,128)(2,1)} copy(bf16[2,16,32,1024]{3,2,0,1:T(8,128)(2,1)} %bitcast.196) | data formatting | bytes 4194304 | tf_op jit(solution)/shard_map/transpose | solution.py:30
  212.7 5.7 %convolution_convert_fusion.1 = bf16[256,3072]{1,0:T(8,128)(2,1)} fusion(bf16[256,1024]{1,0:T(8,128)(2,1)S(1)} %reshape.273, bf16[1024,3072]{1,0:T(8,128)(2,1)} %bitcast.193), kind=kOutput, calls=%fused_computation.5 | convolution fusion | flops 1611399168 | bytes 8388608 | tf_op jit(solution)/shard_map/dot_general | solution.py:106
  218.4 3.6 %reshape_reshape.19 = bf16[2,64,1,2,3,16,64]{6,5,4,3,1,0,2:T(8,128)(2,1)S(1)} reshape(bf16[256,3072]{1,0:T(8,128)(2,1)} %convolution_convert_fusion.1) | data formatting | bytes 3145728 | tf_op jit(solution)/shard_map/reshape;reshape | solution.py:77
  222.1 2.0 fusion.41
  224.1 3.1 %copy.190 = bf16[2,64,1,2,1,16,64]{1,6,5,3,0,4,2:T(8,128)(2,1)} copy(bf16[2,64,1,2,1,16,64]{6,5,4,3,1,0,2:T(8,128)(2,1)} %get-tuple-element.5) | data formatting | bytes 1048576
  227.1 3.7 %fusion.49 = (f32[2,2,16,64]{3,2,1,0:T(8,128)S(1)}, f32[2,2,16,64,64]{3,4,2,1,0:T(8,128)}) fusion(f32[16,64,64]{1,2,0:T(8,128)} %copy.146, bf16[2,64,1,2,1,16,64]{6,5,4,3,1,0,2:T(8,128)(2,1)S(1)} %copy-done.9, bf16[2,64,1,2,1,16,64]{6,5,4,3,1,0,2:T(8,128)(2,1)S(1)} %copy-done.10), kind=kOutput, calls=%fused_computation.96 | convolution fusion | flops 34603072 | bytes 2375680 | tf_op jit(solution)/shard_map/sub | solution.py:85
  231.1 0.3 concatenate.15
  231.4 1.4 copy.175
  232.8 0.2 copy.174
  233.1 0.3 concatenate.16
  233.4 1.4 copy.176
  234.8 1.6 convert_bitcast_fusion.1
  236.5 1.1 reshape.290
  237.6 2.2 copy.157
  239.9 4.0 %fusion.6 = bf16[2,64,1,2,16,64]{1,5,4,3,0,2:T(8,128)(2,1)} fusion(f32[2,64,1,2,16,64]{1,5,4,3,0,2:T(8,128)} %copy.157, f32[2,2,16,64,64]{3,4,2,1,0:T(8,128)} %get-tuple-element.26, bf16[1,64,1,2,16,64]{1,5,4,3,0,2:T(8,128)(2,1)} %copy.176, bf16[1,64,1,2,16,64]{1,5,4,3,0,2:T(8,128)(2,1)} %copy.175, bf16[2,64,1,2,1,16,64]{1,6,5,3,0,4,2:T(8,128)(2,1)S(1)} %copy-done.5, ...), kind=kOutput, calls=%fused_computation.11 | convolution fusion | flops 35913728 | bytes 3686400 | tf_op jit(solution)/shard_map/byzhxw,bwyzhs->bxyzhs/dot_general | solution.py:88
  243.9 2.7 %copy.177 = bf16[2,64,1,2,16,64]{5,4,3,1,0,2:T(8,128)(2,1)S(1)} copy(bf16[2,64,1,2,16,64]{1,5,4,3,0,2:T(8,128)(2,1)} %fusion.6) | data formatting | bytes 1048576 | tf_op jit(solution)/shard_map/convert_element_type | solution.py:122
  246.6 1.5 convert_element_type.194
  248.1 2.1 fusion.18
  250.3 1.0 reshape.288
  (52 shorter events, 2.2 us)
Async XLA Ops:
  6.5 196.2 %copy-start = (f32[16,127]{1,0:T(8,128)S(1)}, f32[16,127]{1,0:T(8,128)}, u32[]{:S(2)}) copy-start(f32[16,127]{1,0:T(8,128)} %param.9) | copy-start | bytes 24388
  6.5 13.1 %copy-start.2 = (bf16[2,64,1,2,1024]{4,3,2,1,0:T(2,128)(2,1)S(1)}, bf16[2,64,1,2,1024]{4,3,2,1,0:T(2,128)(2,1)}, u32[]{:S(2)}) copy-start(bf16[2,64,1,2,1024]{4,3,2,1,0:T(2,128)(2,1)} %param.6) | copy-start | bytes 1572868
  6.5 121.3 %all-gather.5.cloned.1.call-start = ((), (), s32[]{:S(2)}) async-start(), calls=%async_computation.6 | async-start | bytes 6684672 | tf_op jit(solution)/shard_map/all_gather | solution.py:26
  19.7 44.5 %copy-start.12 = (bf16[32,1024]{1,0:T(8,128)(2,1)S(1)}, bf16[32,1024]{1,0:T(8,128)(2,1)}, u32[]{:S(2)}) copy-start(bf16[32,1024]{1,0:T(8,128)(2,1)} %param.8) | copy-start | bytes 196612
  19.7 49.9 %copy-start.13 = (f32[16,63]{1,0:T(8,128)S(1)}, f32[16,63]{1,0:T(8,128)}, u32[]{:S(2)}) copy-start(f32[16,63]{1,0:T(8,128)} %param.11) | copy-start | bytes 12100
  21.1 49.8 %copy-start.14 = (f32[16,63]{1,0:T(8,128)S(1)}, f32[16,63]{1,0:T(8,128)}, u32[]{:S(2)}) copy-start(f32[16,63]{1,0:T(8,128)} %param.10) | copy-start | bytes 12100
  48.3 54.2 %all-to-all-start = ((bf16[2,64,1,2,1024]{4,3,2,0,1:T(2,128)(2,1)}), bf16[2,64,1,2,1024]{4,3,2,0,1:T(2,128)(2,1)S(1)}, u32[]{:S(2)}, u32[]{:S(2)}) async-start(bf16[2,64,1,2,1024]{4,3,2,0,1:T(2,128)(2,1)} %multiply_convert_fusion), calls=%async_computation | async-start | bytes 1048576 | tf_op jit(solution)/shard_map/all_to_all | solution.py:117
  64.1 145.3 %all-gather.7.cloned.1.call-start = ((), (), s32[]{:S(2)}) async-start(), calls=%async_computation.7 | async-start | bytes 2228224 | tf_op jit(solution)/shard_map/all_gather | solution.py:26
  71.0 66.1 %copy-start.11 = (f32[16,32,32]{1,2,0:T(8,128)}, f32[16,32,32]{1,2,0:T(8,128)S(1)}, u32[]{:S(2)}) copy-start(f32[16,32,32]{1,2,0:T(8,128)S(1)} %copy.162) | copy-start | bytes 196612
  131.1 2.7 %copy-start.1 = (bf16[2,16,32,3072]{3,2,1,0:T(8,128)(2,1)}, bf16[2,16,32,3072]{3,2,1,0:T(8,128)(2,1)S(1)}, u32[]{:S(2)}) copy-start(bf16[2,16,32,3072]{3,2,1,0:T(8,128)(2,1)S(1)} %copy.142) | copy-start | bytes 18874372
  142.8 35.6 %all-to-all-start.3 = ((bf16[1,4,1,32,1024]{4,1,2,0,3:T(4,128)(2,1)}), bf16[1,4,1,32,1024]{4,1,2,0,3:T(4,128)(2,1)S(1)}, u32[]{:S(2)}, u32[]{:S(2)}) async-start(bf16[1,4,1,32,1024]{4,1,2,0,3:T(4,128)(2,1)} %reshape.299), calls=%async_computation.3 | async-start | bytes 524288 | tf_op jit(solution)/shard_map/all_to_all | solution.py:97
  174.0 10.0 %copy-start.8 = (bf16[2,2,32,2,1,16,64]{6,5,4,3,2,1,0:T(8,128)(2,1)S(1)}, bf16[2,2,32,2,1,16,64]{6,5,4,3,2,1,0:T(8,128)(2,1)}, u32[]{:S(2)}) copy-start(bf16[2,2,32,2,1,16,64]{6,5,4,3,2,1,0:T(8,128)(2,1)} %get-tuple-element.8) | copy-start | bytes 1572868
  178.3 12.9 %all-to-all-start.5 = ((bf16[1,4,1,32,1024]{4,1,2,0,3:T(4,128)(2,1)}), bf16[1,4,1,32,1024]{4,1,2,0,3:T(4,128)(2,1)S(1)}, u32[]{:S(2)}, u32[]{:S(2)}) async-start(bf16[1,4,1,32,1024]{4,1,2,0,3:T(4,128)(2,1)} %reshape.300), calls=%async_computation.5 | async-start | bytes 524288 | tf_op jit(solution)/shard_map/all_to_all | solution.py:97
  191.2 15.8 %copy-start.6 = (bf16[1,4,1,32,1024]{4,1,2,0,3:T(4,128)(2,1)}, bf16[1,4,1,32,1024]{4,1,2,0,3:T(4,128)(2,1)S(1)}, u32[]{:S(2)}) copy-start(bf16[1,4,1,32,1024]{4,1,2,0,3:T(4,128)(2,1)S(1)} %all-to-all-done.5) | copy-start | bytes 786436
  191.2 43.6 %all-to-all-start.1 = ((bf16[2,2,32,2,1024]{4,3,1,0,2:T(2,128)(2,1)}), bf16[2,2,32,2,1024]{4,3,1,0,2:T(2,128)(2,1)}, u32[]{:S(2)}, u32[]{:S(2)}) async-start(bf16[2,2,32,2,1024]{4,3,1,0,2:T(2,128)(2,1)} %reshape.298), calls=%async_computation.1 | async-start | bytes 1048576 | tf_op jit(solution)/shard_map/all_to_all | solution.py:93
  201.1 6.0 %copy-start.3 = (bf16[2,64,1,2,1024]{4,3,2,1,0:T(2,128)(2,1)S(1)}, bf16[2,64,1,2,1024]{4,3,2,1,0:T(2,128)(2,1)}, u32[]{:S(2)}) copy-start(bf16[2,64,1,2,1024]{4,3,2,1,0:T(2,128)(2,1)} %param.6) | copy-start | bytes 1572868
  224.0 3.1 %copy-start.9 = (bf16[2,64,1,2,1,16,64]{6,5,4,3,1,0,2:T(8,128)(2,1)S(1)}, bf16[2,64,1,2,1,16,64]{6,5,4,3,1,0,2:T(8,128)(2,1)}, u32[]{:S(2)}) copy-start(bf16[2,64,1,2,1,16,64]{6,5,4,3,1,0,2:T(8,128)(2,1)} %get-tuple-element.6) | copy-start | bytes 1572868
  224.1 3.1 %copy-start.10 = (bf16[2,64,1,2,1,16,64]{6,5,4,3,1,0,2:T(8,128)(2,1)S(1)}, bf16[2,64,1,2,1,16,64]{6,5,4,3,1,0,2:T(8,128)(2,1)}, u32[]{:S(2)}) copy-start(bf16[2,64,1,2,1,16,64]{6,5,4,3,1,0,2:T(8,128)(2,1)} %get-tuple-element.7) | copy-start | bytes 1572868
  230.8 2.0 copy-start.7
  237.6 2.3 copy-start.5
  243.9 4.3 %copy-start.4 = (bf16[2,16,32,1024]{3,2,1,0:T(8,128)(2,1)S(1)}, bf16[2,16,32,1024]{3,2,1,0:T(8,128)(2,1)}, u32[]{:S(2)}) copy-start(bf16[2,16,32,1024]{3,2,1,0:T(8,128)(2,1)} %copy.178) | copy-start | bytes 6291460
Sparse Core Ops, SparseCore 0:
  16.2 111.6 all-gather.4
  129.9 63.7 all-gather.6
where the time goes:
time: 259 us; the launch traced here: 258 us
  waiting for transfers between devices  56.7 us (22%)
  local copies, waits for them, and re-layouts  53 us (20%)
  matrix products  47.2 us (18%)
  blocking collectives  40.7 us (16%)
  starting transfers between devices  39.6 us (15%)
  between operations  13.8 us (5%)
  other arithmetic  7.16 us (3%)
    all_to_all x1, waiting for transfers between devices, shards(): lax.all_to_all(normed, GY, split_axis=1, concat_axis=2, tiled=True)  28.8 us
    all_to_all x2, blocking collectives, moved(): lax.all_to_all(group, axis, split_axis=split_dim, concat_axis=concat_dim,...  25.8 us
    all_gather x2, waiting for transfers between devices, stacked_from(): tiles = lax.all_gather(tiles, axes[k], axis=0, tiled=True)  24.8 us
    dot_general x4, matrix products, project(): jnp.dot(inputs.reshape(-1, features), gathered, preferred_element_type=jn...  16.4 us
    all_to_all x1, starting transfers between devices, shards(): lax.all_to_all(normed, GY, split_axis=1, concat_axis=2, tiled=True)  15.8 us
    all_gather x2, blocking collectives, stacked_from(): tiles = lax.all_gather(tiles, axes[k], axis=0, tiled=True)  14.9 us
    all_to_all x2, starting transfers between devices, return_z(): return lax.all_to_all(result, 'gz', split_axis=3, concat_axis=1, tiled=True)  13.9 us
    sub x4, matrix products, attend(): scores = scores - jnp.max(scores, axis=-1, keepdims=True)  13.6 us
  transfers between devices with their start and end apart: 6, of which 3 were waited for; matrix products, arithmetic and copies ran while one was open for 34% of the time, Pallas kernels for 0%

commit v1 on v0

--- a/solution.py
+++ b/solution.py
@@ -23,7 +23,9 @@
 def stacked_from(shard, axes, sequence):
     tiles = shard[None]
     for k in sequence:
-        tiles = lax.all_gather(tiles, axes[k], axis=0, tiled=True)
+        tiles = jnp.concatenate(
+            lax.all_to_all(jnp.stack([tiles] * lax.axis_size(axes[k])), axes[k], 0, 0), axis=0
+        )
     held = [lax.axis_size(axes[k]) for k in reversed(sequence)]
     tiles = tiles.reshape(*held, *shard.shape)
     turned = sorted(range(len(sequence)), key=lambda place: sequence[len(sequence) - 1 - place])

time: 259 us -> 562 us (2.17)
  blocking collectives: 40.7 us -> 347 us
  between operations: 13.8 us -> 0.44 us
    all_to_all x0 -> x2, blocking collectives: none -> 320 us  [the longest x1 275 us: stacked_from(): lax.all_to_all(jnp.stack([tiles] * lax.axis_size(axes[k])), axes[k], 0, 0)]
    all_to_all x1 -> x3, waiting for transfers between devices: 28.8 us -> 55.6 us  [stacked_from(): lax.all_to_all(jnp.stack([tiles] * lax.axis_size(axes[k])), axes[k], 0, 0)]
    all_gather x2 -> x0, waiting for transfers between devices: 24.8 us -> none  [stacked_from(): tiles = lax.all_gather(tiles, axes[k], axis=0, tiled=True)]
    all_gather x2 -> x0, blocking collectives: 14.9 us -> none  [stacked_from(): tiles = lax.all_gather(tiles, axes[k], axis=0, tiled=True)]
    transpose x2 -> x0, local copies, waits for them, and re-layouts: 6.46 us -> none  [stacked_from(): tiles.transpose(*turned, *range(len(sequence), tiles.ndim))]
    all_to_all x0 -> x2, local copies, waits for them, and re-layouts: none -> 6.45 us  [stacked_from(): lax.all_to_all(jnp.stack([tiles] * lax.axis_size(axes[k])), axes[k], 0, 0)]
    all_to_all x1 -> x3, starting transfers between devices: 15.8 us -> 21.6 us  [stacked_from(): lax.all_to_all(jnp.stack([tiles] * lax.axis_size(axes[k])), axes[k], 0, 0)]
  transfers between devices with their start and end apart: 6 -> 6, of which waited for: 3 -> 4; matrix products, arithmetic and copies ran while one was open for 34% -> 15% of each run, Pallas kernels for 0% -> 0%
where the time goes in v1:
time: 562 us; the launch traced here: 560 us
  blocking collectives  347 us (62%)
  waiting for transfers between devices  61.7 us (11%)
  local copies, waits for them, and re-layouts  53.2 us (9%)
  matrix products  46.8 us (8%)
  starting transfers between devices  42.2 us (8%)
  other arithmetic  8.72 us (2%)
    all_to_all x1, blocking collectives, stacked_from(): lax.all_to_all(jnp.stack([tiles] * lax.axis_size(axes[k])), axes[k], 0, 0)  275 us
    all_to_all x3, waiting for transfers between devices, stacked_from(): lax.all_to_all(jnp.stack([tiles] * lax.axis_size(axes[k])), axes[k], 0, 0)  55.6 us
    all_to_all x1, blocking collectives, shards(): lax.all_to_all(normed, GY, split_axis=1, concat_axis=2, tiled=True)  45.2 us
    all_to_all x2, blocking collectives, moved(): lax.all_to_all(group, axis, split_axis=split_dim, concat_axis=concat_dim,...  27 us
    all_to_all x3, starting transfers between devices, stacked_from(): lax.all_to_all(jnp.stack([tiles] * lax.axis_size(axes[k])), axes[k], 0, 0)  21.6 us
    dot_general x4, matrix products, project(): jnp.dot(inputs.reshape(-1, features), gathered, preferred_element_type=jn...  16.3 us
    sub x4, matrix products, attend(): scores = scores - jnp.max(scores, axis=-1, keepdims=True)  13.3 us
    all_to_all x2, starting transfers between devices, return_z(): return lax.all_to_all(result, 'gz', split_axis=3, concat_axis=1, tiled=True)  12.9 us
  transfers between devices with their start and end apart: 6, of which 4 were waited for; matrix products, arithmetic and copies ran while one was open for 15% of the time, Pallas kernels for 0%

profile of v1, /device:TPU:1, one launch (start us, length us, event | category | flops | bytes accessed | tf_op | source)
XLA Modules:
  0.0 560.4 jit_solution(12601702568449260412)
XLA Ops:
  0.0 1.6 pad_maximum_fusion.1
  1.6 5.0 all-to-all-start.8
  6.6 1.6 convert_reduce_fusion
  8.2 1.9 multiply_reduce_fusion
  10.2 0.8 pad_maximum_fusion
  11.0 0.6 multiply_convert_fusion
  11.7 4.2 all-to-all-start
  16.3 5.9 %all-to-all-done = bf16[2,1,32,3072]{3,2,1,0:T(8,128)(2,1)S(1)} async-done(((bf16[2,1,32,3072]{3,2,1,0:T(8,128)(2,1)}), bf16[2,1,32,3072]{3,2,1,0:T(8,128)(2,1)S(1)}, u32[]{:S(2)}, u32[]{:S(2)}) %all-to-all-start) | async-done | bytes 393248 | tf_op jit(solution)/shard_map/all_to_all | solution.py:27
  22.1 16.6 %all_to_all.104 = bf16[1,64,1,2,1024]{4,3,2,0,1:T(2,128)(2,1)S(1)} all-to-all(bf16[1,64,1,2,1024]{4,3,2,0,1:T(2,128)(2,1)S(1)} %get-tuple-element.17), channel_id=1, replica_groups=mesh['gy_0'=2,'gy_1'=16,'gz'=16] {'gz'}, dimensions={1} | all-to-all | bytes 524288 | tf_op jit(solution)/shard_map/all_to_all | solution.py:42
  38.7 10.5 %all_to_all.105 = bf16[1,64,1,2,1024]{4,3,2,0,1:T(2,128)(2,1)S(1)} all-to-all(bf16[1,64,1,2,1024]{4,3,2,0,1:T(2,128)(2,1)S(1)} %get-tuple-element.18), channel_id=1, replica_groups=mesh['gy_0'=2,'gy_1'=16,'gz'=16] {'gz'}, dimensions={1} | all-to-all | bytes 524288 | tf_op jit(solution)/shard_map/all_to_all | solution.py:42
  49.2 45.2 %all_to_all.106 = bf16[2,64,1,2,1024]{4,3,2,0,1:T(2,128)(2,1)S(1)} all-to-all(bf16[2,64,1,2,1024]{4,3,2,0,1:T(2,128)(2,1)S(1)} %multiply_convert_fusion), channel_id=1, replica_groups=mesh['gy_0'=2,'gy_1'=16,'gz'=16] {'gy_0','gy_1'}, dimensions={1} | all-to-all | bytes 1048576 | tf_op jit(solution)/shard_map/all_to_all | solution.py:119
  94.3 0.8 stack.13
  95.1 275.2 %all_to_all.107 = bf16[16,2,32,3072]{3,2,1,0:T(8,128)(2,1)} all-to-all(bf16[16,2,32,3072]{3,2,1,0:T(8,128)(2,1)S(1)} %stack.13), channel_id=1, replica_groups=mesh['gy_0'=2,'gy_1'=16,'gz'=16] {'gy_1'}, dimensions={0} | all-to-all | bytes 12582912 | tf_op jit(solution)/shard_map/all_to_all | solution.py:27
  370.3 1.6 stack.15
  372.0 12.3 %all-to-all-start.9 = ((bf16[16,2,32,1024]{3,2,1,0:T(8,128)(2,1)}), bf16[16,2,32,1024]{3,2,1,0:T(8,128)(2,1)}, u32[]{:S(2)}, u32[]{:S(2)}) async-start(bf16[16,2,32,1024]{3,2,1,0:T(8,128)(2,1)} %stack.15), calls=%async_computation.9 | async-start | bytes 4194304 | tf_op jit(solution)/shard_map/all_to_all | solution.py:27
  384.3 1.2 convolution_bitcast_fusion
  385.7 1.2 convolution_bitcast_fusion.1
  386.9 0.9 copy.115
  388.9 3.2 copy.105
  392.2 2.6 copy-done.1
  394.8 1.0 convolution_convert_fusion.3
  395.8 1.0 reshape_reshape.21
  396.8 1.3 fusion.43
  398.2 2.8 fusion.48
  400.9 1.6 fusion.20
  402.7 1.0 reshape.293
  403.8 3.8 convolution_convert_fusion.2
  407.5 1.0 reshape_reshape.22
  408.6 1.2 fusion.44
  409.7 2.6 fusion.47
  412.4 1.6 fusion.21
  414.2 1.0 reshape.294
  415.1 5.8 %convolution_convert_fusion = bf16[256,3072]{1,0:T(8,128)(2,1)} fusion(bf16[256,1024]{1,0:T(8,128)(2,1)S(1)} %reshape.275, bf16[1024,3072]{1,0:T(8,128)(2,1)} %bitcast.192), kind=kOutput, calls=%fused_computation.4 | convolution fusion | flops 1611399168 | bytes 8388608 | tf_op jit(solution)/shard_map/dot_general | solution.py:108
  420.9 3.6 reshape_reshape.20
  424.5 2.0 fusion.42
  426.5 49.7 %all-to-all-done.9 = bf16[16,2,32,1024]{3,2,1,0:T(8,128)(2,1)} async-done(((bf16[16,2,32,1024]{3,2,1,0:T(8,128)(2,1)}), bf16[16,2,32,1024]{3,2,1,0:T(8,128)(2,1)}, u32[]{:S(2)}, u32[]{:S(2)}) %all-to-all-start.9) | async-done | bytes 2097184 | tf_op jit(solution)/shard_map/all_to_all | solution.py:27
  476.2 8.8 %all-to-all-start.5 = ((bf16[1,4,1,32,1024]{4,1,2,0,3:T(4,128)(2,1)}), bf16[1,4,1,32,1024]{4,1,2,0,3:T(4,128)(2,1)S(1)}, u32[]{:S(2)}, u32[]{:S(2)}) async-start(bf16[1,4,1,32,1024]{4,1,2,0,3:T(4,128)(2,1)} %reshape.293), calls=%async_computation.5 | async-start | bytes 524288 | tf_op jit(solution)/shard_map/all_to_all | solution.py:99
  485.0 4.3 fusion.46
  489.3 3.0 all-to-all-done.5
  492.2 4.1 all-to-all-start.7
  496.4 2.3 fusion.13
  499.1 1.4 reshape.292
  500.5 3.1 all-to-all-done.7
  503.6 7.7 %all-to-all-start.3 = ((bf16[2,2,32,2,1024]{4,3,1,0,2:T(2,128)(2,1)}), bf16[2,2,32,2,1024]{4,3,1,0,2:T(2,128)(2,1)}, u32[]{:S(2)}, u32[]{:S(2)}) async-start(bf16[2,2,32,2,1024]{4,3,1,0,2:T(2,128)(2,1)} %reshape.292), calls=%async_computation.3 | async-start | bytes 1048576 | tf_op jit(solution)/shard_map/all_to_all | solution.py:95
  511.9 3.2 fusion.19
  515.1 1.1 copy.109
  516.2 0.6 copy_convert_fusion
  516.8 1.7 reshape.285
  518.6 3.2 copy.141
  521.8 5.8 %convolution_convert_fusion.1 = bf16[256,3072]{1,0:T(8,128)(2,1)} fusion(bf16[256,1024]{1,0:T(8,128)(2,1)S(1)} %reshape.271, bf16[1024,3072]{1,0:T(8,128)(2,1)} %bitcast.193), kind=kOutput, calls=%fused_computation.5 | convolution fusion | flops 1611399168 | bytes 8388608 | tf_op jit(solution)/shard_map/dot_general | solution.py:108
  527.5 3.6 reshape_reshape.19
  531.2 2.0 fusion.41
  533.2 3.1 copy.153
  536.2 3.7 fusion.49
  540.5 1.4 copy.138
  542.5 1.4 copy.139
  543.9 1.6 convert_bitcast_fusion.1
  545.6 1.1 reshape.286
  546.7 2.2 copy.120
  549.0 4.0 fusion.6
  553.0 2.7 copy.140
  555.7 1.5 convert_element_type.194
  557.2 2.1 fusion.18
  559.4 1.0 reshape.284
  (56 shorter events, 4.5 us)
Async XLA Ops:
  0.0 511.9 %copy-start = (f32[16,127]{1,0:T(8,128)S(1)}, f32[16,127]{1,0:T(8,128)}, u32[]{:S(2)}) copy-start(f32[16,127]{1,0:T(8,128)} %param.9) | copy-start | bytes 24388
  0.0 11.0 %copy-start.2 = (bf16[2,64,1,2,1024]{4,3,2,1,0:T(2,128)(2,1)S(1)}, bf16[2,64,1,2,1024]{4,3,2,1,0:T(2,128)(2,1)}, u32[]{:S(2)}) copy-start(bf16[2,64,1,2,1024]{4,3,2,1,0:T(2,128)(2,1)} %param.6) | copy-start | bytes 1572868
  0.0 10.2 %copy-start.13 = (bf16[32,3072]{1,0:T(8,128)(2,1)S(1)}, bf16[32,3072]{1,0:T(8,128)(2,1)}, u32[]{:S(2)}) copy-start(bf16[32,3072]{1,0:T(8,128)(2,1)} %param.7) | copy-start | bytes 589828
  1.6 10.0 %all-to-all-start.8 = ((bf16[2,1,32,1024]{3,2,1,0:T(8,128)(2,1)}), bf16[2,1,32,1024]{3,2,1,0:T(8,128)(2,1)S(1)}, u32[]{:S(2)}, u32[]{:S(2)}) async-start(bf16[2,1,32,1024]{3,2,1,0:T(8,128)(2,1)} %pad_maximum_fusion.1), calls=%async_computation.8 | async-start | bytes 262144 | tf_op jit(solution)/shard_map/all_to_all | solution.py:27
  11.6 83.5 %copy-start.5 = (bf16[2,64,1,2,1024]{4,3,2,0,1:T(2,128)(2,1)}, bf16[2,64,1,2,1024]{4,3,2,0,1:T(2,128)(2,1)S(1)}, u32[]{:S(2)}) copy-start(bf16[2,64,1,2,1024]{4,3,2,0,1:T(2,128)(2,1)S(1)} %multiply_convert_fusion) | copy-start | bytes 1572868
  11.7 10.5 %all-to-all-start = ((bf16[2,1,32,3072]{3,2,1,0:T(8,128)(2,1)}), bf16[2,1,32,3072]{3,2,1,0:T(8,128)(2,1)S(1)}, u32[]{:S(2)}, u32[]{:S(2)}) async-start(bf16[2,1,32,3072]{3,2,1,0:T(8,128)(2,1)} %pad_maximum_fusion), calls=%async_computation | async-start | bytes 786432 | tf_op jit(solution)/shard_map/all_to_all | solution.py:27
  371.9 12.4 %copy-start.14 = (f32[16,63]{1,0:T(8,128)S(1)}, f32[16,63]{1,0:T(8,128)}, u32[]{:S(2)}) copy-start(f32[16,63]{1,0:T(8,128)} %param.11) | copy-start | bytes 12100
  371.9 13.7 %copy-start.15 = (f32[16,63]{1,0:T(8,128)S(1)}, f32[16,63]{1,0:T(8,128)}, u32[]{:S(2)}) copy-start(f32[16,63]{1,0:T(8,128)} %param.10) | copy-start | bytes 12100
  372.0 104.2 %all-to-all-start.9 = ((bf16[16,2,32,1024]{3,2,1,0:T(8,128)(2,1)}), bf16[16,2,32,1024]{3,2,1,0:T(8,128)(2,1)}, u32[]{:S(2)}, u32[]{:S(2)}) async-start(bf16[16,2,32,1024]{3,2,1,0:T(8,128)(2,1)} %stack.15), calls=%async_computation.9 | async-start | bytes 4194304 | tf_op jit(solution)/shard_map/all_to_all | solution.py:27
  392.2 2.7 copy-start.1
  476.2 16.0 %all-to-all-start.5 = ((bf16[1,4,1,32,1024]{4,1,2,0,3:T(4,128)(2,1)}), bf16[1,4,1,32,1024]{4,1,2,0,3:T(4,128)(2,1)S(1)}, u32[]{:S(2)}, u32[]{:S(2)}) async-start(bf16[1,4,1,32,1024]{4,1,2,0,3:T(4,128)(2,1)} %reshape.293), calls=%async_computation.5 | async-start | bytes 524288 | tf_op jit(solution)/shard_map/all_to_all | solution.py:99
  485.0 11.4 %copy-start.10 = (bf16[2,2,32,2,1,16,64]{6,5,4,3,2,1,0:T(8,128)(2,1)S(1)}, bf16[2,2,32,2,1,16,64]{6,5,4,3,2,1,0:T(8,128)(2,1)}, u32[]{:S(2)}) copy-start(bf16[2,2,32,2,1,16,64]{6,5,4,3,2,1,0:T(8,128)(2,1)} %get-tuple-element.8) | copy-start | bytes 1572868
  492.2 11.4 %all-to-all-start.7 = ((bf16[1,4,1,32,1024]{4,1,2,0,3:T(4,128)(2,1)}), bf16[1,4,1,32,1024]{4,1,2,0,3:T(4,128)(2,1)S(1)}, u32[]{:S(2)}, u32[]{:S(2)}) async-start(bf16[1,4,1,32,1024]{4,1,2,0,3:T(4,128)(2,1)} %reshape.294), calls=%async_computation.7 | async-start | bytes 524288 | tf_op jit(solution)/shard_map/all_to_all | solution.py:99
  498.7 12.6 %copy-start.6 = (bf16[2,64,1,2,1024]{4,3,2,0,1:T(2,128)(2,1)S(1)}, bf16[2,64,1,2,1024]{4,3,2,0,1:T(2,128)(2,1)}, u32[]{:S(2)}) copy-start(bf16[2,64,1,2,1024]{4,3,2,0,1:T(2,128)(2,1)} %copy-done.5) | copy-start | bytes 1572868
  503.6 12.6 %copy-start.8 = (bf16[1,4,1,32,1024]{4,1,2,0,3:T(4,128)(2,1)}, bf16[1,4,1,32,1024]{4,1,2,0,3:T(4,128)(2,1)S(1)}, u32[]{:S(2)}) copy-start(bf16[1,4,1,32,1024]{4,1,2,0,3:T(4,128)(2,1)S(1)} %all-to-all-done.7) | copy-start | bytes 786436
  503.6 40.3 %all-to-all-start.3 = ((bf16[2,2,32,2,1024]{4,3,1,0,2:T(2,128)(2,1)}), bf16[2,2,32,2,1024]{4,3,1,0,2:T(2,128)(2,1)}, u32[]{:S(2)}, u32[]{:S(2)}) async-start(bf16[2,2,32,2,1024]{4,3,1,0,2:T(2,128)(2,1)} %reshape.292), calls=%async_computation.3 | async-start | bytes 1048576 | tf_op jit(solution)/shard_map/all_to_all | solution.py:95
  511.3 4.9 copy-start.3
  533.2 3.1 copy-start.11
  533.2 3.1 copy-start.12
  539.9 2.0 copy-start.9
  546.7 2.3 copy-start.7
  553.0 4.3 copy-start.4
